TPU v7x, 32 devices: a whole 2x2x4 slice. The times are simulated.
32 devices in a mesh: groups: 2 (over y), tp: 4 (over z), pd: 4 (over x, core).
Axes of the slice: x: 2, y: 2, z: 4, core: 2. Of those that a mesh axis runs over, the one named last changes fastest.
Arguments:
- prefill_hidden: bfloat16 [49152, 7168], P(('groups', 'pd'), 'tp'), parts along dimension 0, may hold values from -6 to 6
- draft_hidden: bfloat16 [64, 7168], P(('groups', 'pd'), 'tp'), parts along dimension 0, may hold values from -6 to 6
- kv_down: bfloat16 [7168, 576], P('tp'), may hold values from -0.0625 to 0.0625
- kv_gain: float32 [512], replicated, may hold values from 0.1 to 1.9
- query_latent: bfloat16 [32, 2, 1536], P('groups'), parts along dimension 0, may hold values from -110 to 110, as said below
- q_up: bfloat16 [1536, 24576], P(None, 'tp'), may hold values from -0.15625 to 0.15625
- kv_up: bfloat16 [512, 32768], P(None, 'tp'), may hold values from -0.25 to 0.25
- owners: int32 [32], P('groups'), parts along dimension 0, may hold values from 0 to 3, as said below
- segment_ids: int32 [32, 1536], P('groups'), parts along dimension 0, may hold values from 0 to 3, never falling along the last dimension, each value on 1 to 768 neighbouring positions
- accepted: int32 [32], P('groups'), parts along dimension 0, may hold values from 0 to 1
Outputs:
- owner_decoded: bfloat16 [64, 16384], P(('groups', 'pd'), 'tp'), parts along dimension 0
- owner_cache: bfloat16 [32, 1536, 576], P(('groups', 'pd'), 'tp'), parts along dimension 0
There are 2 independent parts, one for each index of `groups`. A program takes and returns all parts, laid end to end along the dimension named above; an argument that names none is the same for every part. Nothing has to cross between parts.
Inputs may be any that keep to these rules, and one draw needn't show every extreme that they name: Owners are pd indices. Requests p * 4 to p * 4 + 3 belong to prefill rank p, and those 4 requests have 4 different owners; one owner holds a request of every prefill rank. `query_latent`: A few new tokens may have large query latents.
All inputs are finite; a program needn't handle non-finite values.
Results may differ from a plain program's by a relative error of at most 0.0117.
The roundings to bfloat16 on the way count: a program that leaves them out, or rounds other values in their place, can miss the bound.
Values may be sent and summed in bfloat16 or wider, within the bound.
No kernel may reach another device: no remote copies, remote signals or barrier semaphores. Data moves between devices by JAX's collectives and lax.ppermute only.
A program may use at most 192 MiB of HBM per device.

v0:
```python
import jax
import jax.numpy as jnp
from jax import lax
from jax.sharding import PartitionSpec as P

DN = 128
DR = 64
DV = 128
KVL = 512
QL = 1536
PRE_TOK = 1536
RP = 4


def rms_latent(comp, gain):
    lat = comp[:, :KVL]
    scale = lax.rsqrt(jnp.mean(lat * lat, axis=-1, keepdims=True) + 1e-06)
    return (lat * scale * gain).astype(jnp.bfloat16)


def rotate(values, position):
    half = values.shape[-1] // 2
    freq = jnp.exp(-jnp.log(10000.0) * jnp.arange(half, dtype=jnp.float32) / half)
    angle = position.astype(jnp.float32)[..., None] * freq
    cosine = jnp.cos(angle)
    sine = jnp.sin(angle)
    first = values[..., :half]
    second = values[..., half:]
    return jnp.concatenate([first * cosine - second * sine, first * sine + second * cosine], -1)


def block_stats(keys, q_lat, q_pos, valid):
    scale = (DN + DR) ** (-0.5)
    scores = jnp.einsum("jhk,tk->jht", q_lat, keys[:, :KVL], preferred_element_type=jnp.float32)
    scores = (
        scores + jnp.einsum("jhk,tk->jht", q_pos, keys[:, KVL:], preferred_element_type=jnp.float32)
    ) * scale
    scores = jnp.where(valid, scores, -1e30)
    top = jnp.max(scores, axis=-1)
    weights = jnp.where(valid, jnp.exp(scores - top[..., None]), 0.0)
    total = jnp.sum(weights, axis=-1)
    numer = jnp.einsum(
        "jht,tk->jhk",
        weights.astype(jnp.bfloat16),
        keys[:, :KVL],
        preferred_element_type=jnp.float32,
    )
    return (top, total, numer)


def combine(left, right):
    top = jnp.maximum(left[0], right[0])
    left_scale = jnp.exp(left[0] - top)
    right_scale = jnp.exp(right[0] - top)
    total = left[1] * left_scale + right[1] * right_scale
    numer = left[2] * left_scale[..., None] + right[2] * right_scale[..., None]
    return (top, total, numer)


def local(
    prefill_hidden,
    draft_hidden,
    kv_down,
    kv_gain,
    query_latent,
    q_up,
    kv_up,
    owners,
    segment_ids,
    accepted,
):
    tp_count = lax.axis_size("tp")
    pd_count = lax.axis_size("pd")
    tp_rank = lax.axis_index("tp")
    mine_rank = lax.axis_index("pd")
    requests = owners.shape[0]
    share = PRE_TOK // tp_count
    width = KVL + DR
    local_hidden = prefill_hidden.reshape(RP, PRE_TOK, prefill_hidden.shape[1])
    summed = lax.psum_scatter(
        jnp.einsum(
            "rtd,dw->trw", local_hidden, kv_down, preferred_element_type=jnp.float32
        ).reshape(lax.axis_size("tp") * share, RP * width),
        "tp",
        scatter_dimension=0,
        tiled=True,
    ).reshape(share * RP, width)
    draft_sum = lax.psum(jnp.dot(draft_hidden, kv_down, preferred_element_type=jnp.float32), "tp")
    first_req = mine_rank * RP
    row_pos = jnp.broadcast_to(
        tp_rank * share + jnp.arange(share, dtype=jnp.int32)[:, None], (share, RP)
    )
    page_rows = jnp.concatenate(
        [
            rms_latent(summed, kv_gain),
            rotate(summed[:, KVL:], row_pos.reshape(-1)).astype(jnp.bfloat16),
        ],
        1,
    )
    page_rows = page_rows.reshape(share, RP, width)
    draft_pos = jnp.tile(PRE_TOK + jnp.arange(2, dtype=jnp.int32), RP)
    draft_rows = jnp.concatenate(
        [
            rms_latent(draft_sum, kv_gain),
            rotate(draft_sum[:, KVL:], draft_pos).astype(jnp.bfloat16),
        ],
        1,
    )
    draft_rows = draft_rows.reshape(RP, 2, width)
    my_owners = lax.dynamic_slice_in_dim(owners, first_req, RP, 0)
    routing = (my_owners[None, :] == jnp.arange(pd_count, dtype=jnp.int32)[:, None]).astype(
        jnp.bfloat16
    )
    send_pages = jnp.einsum(
        "dk,tkw->dtw", routing, page_rows, preferred_element_type=jnp.float32
    ).astype(jnp.bfloat16)
    send_drafts = jnp.einsum(
        "dk,kjw->djw", routing, draft_rows, preferred_element_type=jnp.float32
    ).astype(jnp.bfloat16)
    pages, drafts = (
        lax.all_to_all(send_pages, "pd", split_axis=0, concat_axis=0, tiled=True),
        lax.all_to_all(send_drafts, "pd", split_axis=0, concat_axis=0, tiled=True),
    )
    heads_local = q_up.shape[1] // (DN + DR)
    query_full = jnp.dot(
        query_latent.reshape(requests * 2, QL), q_up, preferred_element_type=jnp.float32
    )
    query_full = query_full.reshape(requests, 2, heads_local, DN + DR)
    new_pos = jnp.broadcast_to(PRE_TOK + jnp.arange(2, dtype=jnp.int32)[None, :], (requests, 2))
    q_nope = query_full[..., :DN].astype(jnp.bfloat16)
    q_rot = rotate(query_full[..., DN:], new_pos[:, :, None]).astype(jnp.bfloat16)
    up_heads = kv_up.reshape(KVL, heads_local, DN + DV)
    w_value = up_heads[:, :, DN:]
    q_abs = jnp.einsum(
        "rjhd,khd->rjhk", q_nope, up_heads[:, :, :DN], preferred_element_type=jnp.float32
    ).astype(jnp.bfloat16)
    owner_table = owners.reshape(pd_count, RP) == mine_rank
    holding = jnp.sum(owner_table.astype(jnp.int32), axis=1)
    slot_of = jnp.sum(
        owner_table.astype(jnp.int32) * jnp.arange(RP, dtype=jnp.int32)[None, :], axis=1
    )
    owned_count = jnp.sum(holding)
    order = jnp.argsort((1 - holding) * pd_count + jnp.arange(pd_count, dtype=jnp.int32))
    draft_valid = (jnp.arange(2)[None, :] <= jnp.arange(2)[:, None])[:, None, :]
    empty = jnp.zeros((pd_count, 2, heads_local * DV), jnp.bfloat16)

    def finish(stats, source, request, q_lat, q_pos, result):
        stats = combine(stats, block_stats(drafts[source], q_lat, q_pos, draft_valid))
        attended = (stats[2] / stats[1][..., None]).astype(jnp.bfloat16)
        head_out = jnp.einsum("jhk,khd->jhd", attended, w_value, preferred_element_type=jnp.float32)
        keep = (jnp.arange(2) <= accepted[request]).astype(jnp.float32)[:, None, None]
        answer = (head_out * keep).astype(jnp.bfloat16).reshape(1, 2, heads_local * DV)
        return lax.dynamic_update_slice(result, answer, (source, 0, 0))

    def attend(turn, result):
        source = order[turn]
        request = source * RP + slot_of[source]
        q_lat = q_abs[request]
        q_pos = q_rot[request]
        seg_row = segment_ids[request]
        current = seg_row[PRE_TOK - 1]
        init = (
            jnp.full((2, heads_local), -1e30, jnp.float32),
            jnp.zeros((2, heads_local), jnp.float32),
            jnp.zeros((2, heads_local, KVL), jnp.float32),
        )
        valid = (seg_row == current)[None, None, :]
        stats = combine(
            init,
            block_stats(
                lax.all_gather(pages[source], "tp", axis=0, tiled=True), q_lat, q_pos, valid
            ),
        )
        return finish(stats, source, request, q_lat, q_pos, result)

    result = lax.fori_loop(0, owned_count, attend, empty)
    return (result.reshape(pd_count * 2, heads_local * DV), pages)


def solution(mesh):
    placed = (
        P(("groups", "pd"), "tp"),
        P(("groups", "pd"), "tp"),
        P("tp", None),
        P(),
        P("groups", None, None),
        P(None, "tp"),
        P(None, "tp"),
        P("groups"),
        P("groups", None),
        P("groups"),
    )
    return jax.shard_map(
        local,
        mesh=mesh,
        in_specs=placed,
        out_specs=(P(("groups", "pd"), "tp"), P(("groups", "pd"), "tp", None)),
        check_vma=False,
    )
```

profile of v0, /device:TPU:16, one launch (start us, length us, event | category | flops | bytes accessed | tf_op | source)
XLA Modules:
  0.0 565.0 jit_solution(5226011808825472450)
XLA Ops:
  7.2 1.5 copy-done
  8.8 20.3 %fusion.43 = f32[576,4,1536]{2,0,1:T(8,128)} fusion(bf16[4,1536,1792]{2,1,0:T(8,128)(2,1)} %bitcast.135, bf16[1792,576]{0,1:T(8,128)(2,1)S(1)} %copy-done), kind=kOutput, calls=%fused_computation.64 | convolution fusion | flops 12683575296 | bytes 38240256 | tf_op jit(solution)/shard_map/rtd,dw->trw/dot_general | solution.py:81
  29.1 15.2 %copy.70 = f32[1536,2304]{1,0:T(8,128)} copy(f32[1536,2304]{0,1:T(8,128)} %bitcast.133) | data formatting | bytes 28311552 | tf_op jit(solution)/shard_map/reshape | solution.py:83
  45.7 18.3 %psum.7 = f32[8,576]{1,0:T(8,128)S(1)} all-reduce(f32[8,576]{1,0:T(8,128)S(1)} %fusion.77), channel_id=1, replica_groups=mesh['groups'=2,'tp'=4,'pd'=4] {'tp'}, use_global_device_ids=true, to_apply=%region_6.0 | all-reduce | flops 4608 | bytes 36864 | tf_op jit(solution)/shard_map/psum | solution.py:88
  65.2 3.4 all-to-all-start.1
  69.0 24.8 %copy.65 = bf16[1536,6144]{0,1:T(8,128)(2,1)} copy(bf16[1536,6144]{1,0:T(8,128)(2,1)} %param.17) | data formatting | bytes 37748736 | tf_op args[5]
  93.7 9.6 %fusion.56 = f32[16,2,32,192]{3,0,2,1:T(8,128)S(1)} fusion(bf16[32,192,1536,1]{2,1,0,3:T(8,128)(2,1)} %bitcast.127, bf16[16,2,1536,1]{2,1,0,3:T(2,128)(2,1)S(1)} %bitcast.134), kind=kOutput, calls=%fused_computation.86 | convolution fusion | flops 603979776 | bytes 19759104 | tf_op jit(solution)/shard_map/dot_general | solution.py:125
  103.3 181.2 %reduce-scatter.2.cloned.1.call-done = f32[384,2304]{1,0:T(8,128)} async-done(((f32[1536,2304]{1,0:T(8,128)}), f32[384,2304]{1,0:T(8,128)}) %reduce-scatter.2.cloned.1.call-update) | async-done | bytes 3538960 | tf_op jit(solution)/shard_map/reduce_scatter | solution.py:80
  284.5 5.5 reshape.178
  290.0 1.6 fusion.76
  291.6 2.2 multiply_reduce_fusion
  295.6 2.2 multiply_convert_fusion
  297.8 1.6 pad_maximum_fusion
  299.4 3.2 reshape.179
  302.6 3.4 copy.75
  306.0 2.5 convolution_convert_fusion
  308.5 1.4 copy.76
  310.0 4.4 all-to-all-start
  315.7 12.0 %copy.67 = bf16[512,8192]{0,1:T(8,128)(2,1)} copy(bf16[512,8192]{1,0:T(8,128)(2,1)} %param.18) | data formatting | bytes 16777216 | tf_op args[6]
  327.6 4.9 slice.96
  332.5 1.2 copy-done.4
  335.1 6.4 %copy.82 = bf16[512,32,128]{2,0,1:T(8,128)(2,1)} copy(bf16[512,32,128]{0,2,1:T(8,128)(2,1)} %slice.96) | data formatting | bytes 8388608
  342.5 212.5 %while.12 = (s32[]{:T(128)}, bf16[4,2,4096]{2,1,0:T(2,128)(2,1)S(1)}, s32[]{:T(128)}, s32[4]{0:T(128)S(1)}, s32[4]{0:T(128)S(1)}, /*index=5*/s32[16,1536]{1,0:T(...) while((s32[]{:T(128)}, ...), condition=%wide.region_13.14_spmd.clone.clone, body=%wide.region_8.13_spmd.clone.clone.sunk | while | flops 223808784 | bytes 42819820 | solution.py:176
  345.4 1.1 constant_dynamic-slice_fusion.2
  349.8 1.3 dynamic-slice.2
  351.0 1.5 compare_reduce_fusion.2
  353.5 37.0 %all-gather.6.cloned.1.call-done = bf16[1,1536,576]{2,1,0:T(8,128)(2,1)} async-done(((bf16[1,384,576]{2,1,0:T(8,128)(2,1)}), bf16[1,1536,576]{2,1,0:T(8,128)(2,1)}) %all-gather.6.cloned.1.call-update) | async-done | bytes 1769488 | tf_op jit(solution)/shard_map/while/body/all_gather | solution.py:171
  390.5 2.1 fusion.106
  392.7 1.5 fusion.107
  398.7 1.1 constant_dynamic-slice_fusion.2
  403.1 1.3 dynamic-slice.2
  404.4 1.5 compare_reduce_fusion.2
  406.9 36.5 %all-gather.6.cloned.1.call-done = bf16[1,1536,576]{2,1,0:T(8,128)(2,1)} async-done(((bf16[1,384,576]{2,1,0:T(8,128)(2,1)}), bf16[1,1536,576]{2,1,0:T(8,128)(2,1)}) %all-gather.6.cloned.1.call-update) | async-done | bytes 1769488 | tf_op jit(solution)/shard_map/while/body/all_gather | solution.py:171
  443.4 2.1 fusion.106
  445.5 1.5 fusion.107
  451.6 1.1 constant_dynamic-slice_fusion.2
  456.0 1.3 dynamic-slice.2
  457.2 1.5 compare_reduce_fusion.2
  459.7 36.5 %all-gather.6.cloned.1.call-done = bf16[1,1536,576]{2,1,0:T(8,128)(2,1)} async-done(((bf16[1,384,576]{2,1,0:T(8,128)(2,1)}), bf16[1,1536,576]{2,1,0:T(8,128)(2,1)}) %all-gather.6.cloned.1.call-update) | async-done | bytes 1769488 | tf_op jit(solution)/shard_map/while/body/all_gather | solution.py:171
  496.2 2.1 fusion.106
  498.4 1.5 fusion.107
  504.4 1.1 constant_dynamic-slice_fusion.2
  508.8 1.3 dynamic-slice.2
  510.1 1.5 compare_reduce_fusion.2
  512.6 36.5 %all-gather.6.cloned.1.call-done = bf16[1,1536,576]{2,1,0:T(8,128)(2,1)} async-done(((bf16[1,384,576]{2,1,0:T(8,128)(2,1)}), bf16[1,1536,576]{2,1,0:T(8,128)(2,1)}) %all-gather.6.cloned.1.call-update) | async-done | bytes 1769488 | tf_op jit(solution)/shard_map/while/body/all_gather | solution.py:171
  549.1 2.1 fusion.106
  551.2 1.5 fusion.107
  555.6 2.9 copy.113
  (139 shorter events, 30.6 us)
Async XLA Ops:
  7.2 1.6 copy-start
  7.2 277.3 %reduce-scatter.2.cloned.1.call-start = ((), (), s32[]{:S(2)}) async-start(), calls=%async_computation.3 | async-start | bytes 17694720 | tf_op jit(solution)/shard_map/reduce_scatter | solution.py:80
  44.3 0.7 copy-start.6
  44.3 19.9 %copy-start.7 = (f32[512]{0:T(512)S(1)}, f32[512]{0:T(512)}, u32[]{:S(2)}) copy-start(f32[512]{0:T(512)} %param.15) | copy-start | bytes 6148
  44.3 20.1 %copy-start.8 = (s32[16]{0:T(128)S(1)}, s32[16]{0:T(128)}, u32[]{:S(2)}) copy-start(s32[16]{0:T(128)} %param.19) | copy-start | bytes 196
  65.2 244.7 %all-to-all-start.1 = ((bf16[4,2,576]{2,1,0:T(2,128)(2,1)}), bf16[4,2,576]{2,1,0:T(2,128)(2,1)S(1)}, u32[]{:S(2)}, u32[]{:S(2)}) async-start(bf16[4,2,576]{2,1,0:T(2,128)(2,1)} %copy.78), calls=%async_computation.2 | async-start | bytes 20480 | tf_op jit(solution)/shard_map/all_to_all | solution.py:122
  68.9 24.8 %copy-start.5 = (bf16[16,2,1536]{2,1,0:T(2,128)(2,1)S(1)}, bf16[16,2,1536]{2,1,0:T(2,128)(2,1)}, u32[]{:S(2)}) copy-start(bf16[16,2,1536]{2,1,0:T(2,128)(2,1)} %param.16) | copy-start | bytes 294916
  310.0 32.5 %all-to-all-start = ((bf16[4,384,576]{1,2,0:T(8,128)(2,1)}), bf16[4,384,576]{1,2,0:T(8,128)(2,1)}, u32[]{:S(2)}, u32[]{:S(2)}) async-start(bf16[4,384,576]{1,2,0:T(8,128)(2,1)} %copy.76), calls=%async_computation.1 | async-start | bytes 3538944 | tf_op jit(solution)/shard_map/all_to_all | solution.py:121
  327.6 6.2 %copy-start.4 = (bf16[512,8192]{0,1:T(8,128)(2,1)S(1)}, bf16[512,8192]{0,1:T(8,128)(2,1)}, u32[]{:S(2)}) copy-start(bf16[512,8192]{0,1:T(8,128)(2,1)} %copy.67) | copy-start | bytes 25165828
  335.1 7.4 %copy-start.9 = (s32[16]{0:T(128)S(1)}, s32[16]{0:T(128)}, u32[]{:S(2)}) copy-start(s32[16]{0:T(128)} %param.21) | copy-start | bytes 196
  343.1 47.5 %all-gather.6.cloned.1.call-start = ((), (), s32[]{:S(2)}) async-start(), calls=%async_computation.4 | async-start | bytes 2457600 | tf_op jit(solution)/shard_map/while/body/all_gather | solution.py:171
  390.5 3.9 copy-start.3
  390.5 4.6 copy-start.2
  396.4 47.0 %all-gather.6.cloned.1.call-start = ((), (), s32[]{:S(2)}) async-start(), calls=%async_computation.4 | async-start | bytes 2457600 | tf_op jit(solution)/shard_map/while/body/all_gather | solution.py:171
  443.4 3.9 copy-start.3
  443.4 4.6 copy-start.2
  449.3 47.0 %all-gather.6.cloned.1.call-start = ((), (), s32[]{:S(2)}) async-start(), calls=%async_computation.4 | async-start | bytes 2457600 | tf_op jit(solution)/shard_map/while/body/all_gather | solution.py:171
  496.2 3.9 copy-start.3
  496.2 4.6 copy-start.2
  502.1 47.0 %all-gather.6.cloned.1.call-start = ((), (), s32[]{:S(2)}) async-start(), calls=%async_computation.4 | async-start | bytes 2457600 | tf_op jit(solution)/shard_map/while/body/all_gather | solution.py:171
  549.1 3.9 copy-start.3
  549.1 4.6 copy-start.2
  554.9 3.5 copy-start.1
Sparse Core Ops, SparseCore 0:
  44.5 239.9 reduce-scatter.1
  347.6 42.9 all-gather.5
  400.9 42.3 all-gather.5
  453.8 42.3 all-gather.5
  506.6 42.3 all-gather.5
where the time goes:
time: 570 us; the launch traced here: 565 us
  waiting for transfers between devices  328 us (58%)
  local copies, waits for them, and re-layouts  109 us (19%)
  matrix products  55.2 us (10%)
  other arithmetic  18.6 us (3%)
  blocking collectives  18.3 us (3%)
  loops' own time  14.5 us (3%)
  between operations  14 us (2%)
  starting transfers between devices  8.04 us (1%)
    reduce_scatter x1, waiting for transfers between devices, local(): lax.psum_scatter(jnp.einsum('rtd,dw->trw', local_hidden, kv_down, preferr...  181 us
    all_gather x4, waiting for transfers between devices, attend(): lax.all_gather(pages[source], 'tp', axis=0, tiled=True)  146 us
    unnamed x24, local copies, waits for them, and re-layouts  50.5 us
    reshape x2, local copies, waits for them, and re-layouts, local(): summed = lax.psum_scatter(jnp.einsum('rtd,dw->trw', local_hidden, kv_down...  20.7 us
    dot_general x1, matrix products, local(): jnp.einsum('rtd,dw->trw', local_hidden, kv_down, preferred_element_type=j...  20.3 us
    psum x1, blocking collectives, local(): lax.psum(jnp.dot(draft_hidden, kv_down, preferred_element_type=jnp.float3...  18.3 us
    another operation x1, loops' own time, local(): result = lax.fori_loop(0, owned_count, attend, empty)  14.5 us
  transfers between devices with their start and end apart: 7, of which 5 were waited for; matrix products, arithmetic and copies ran while one was open for 19% of the time, Pallas kernels for 0%

commit v1 on v0

--- a/solution.py
+++ b/solution.py
@@ -1,6 +1,8 @@
 import jax
 import jax.numpy as jnp
 from jax import lax
+from jax.experimental import pallas as pl
+from jax.experimental.pallas import tpu as pltpu
 from jax.sharding import PartitionSpec as P
 
 DN = 128
@@ -10,6 +12,16 @@
 QL = 1536
 PRE_TOK = 1536
 RP = 4
+WIDTH = KVL + DR
+HALF = DR // 2
+CODED = WIDTH + 16
+UNIT = 128
+LANES = RP * UNIT
+STEPS = 256.0
+TOP = 32767.0
+BF = jnp.bfloat16
+F32 = jnp.float32
+NT = (((1,), (1,)), ((), ()))
 
 
 def rms_latent(comp, gain):
@@ -57,7 +69,7 @@
     return (top, total, numer)
 
 
-def local(
+def local_general(
     prefill_hidden,
     draft_hidden,
     kv_down,
@@ -177,6 +189,459 @@
     return (result.reshape(pd_count * 2, heads_local * DV), pages)
 
 
+def encode(values, out_ref):
+    levels = []
+    for first, last in ((0, KVL), (KVL, WIDTH)):
+        block = values[first:last]
+        top = jnp.maximum(jnp.max(jnp.abs(block), axis=0, keepdims=True), 1e-30)
+        level = jnp.ceil(jnp.log2(top) * STEPS)
+        codes = jnp.round(block * (jnp.exp2(level * (-1.0 / STEPS)) * TOP))
+        codes = jnp.clip(codes, -TOP, TOP).astype(jnp.int32)
+        out_ref[first:last, :] = codes.astype(jnp.int16)
+        levels.append(level.astype(jnp.int32))
+    row = lax.broadcasted_iota(jnp.int32, (16, values.shape[1]), 0)
+    extra = jnp.where(row == 0, levels[0], jnp.where(row == 1, levels[1], 0))
+    out_ref[WIDTH:CODED, :] = extra.astype(jnp.int16)
+
+
+def decode(ref):
+    level = ref[WIDTH:CODED, :].astype(jnp.int32).astype(F32)
+    step = jnp.exp2(level * (1.0 / STEPS)) * (1.0 / TOP)
+    lat = ref[0:KVL, :].astype(jnp.int32).astype(F32) * step[0:1]
+    rot = ref[KVL:WIDTH, :].astype(jnp.int32).astype(F32) * step[1:2]
+    return jnp.concatenate([lat, rot], 0)
+
+
+def key_rows(comp, gain, cosine, sine):
+    lat = comp[:KVL]
+    scale = lax.rsqrt(jnp.mean(lat * lat, axis=0, keepdims=True) + 1e-06)
+    first = comp[KVL : KVL + HALF]
+    second = comp[KVL + HALF :]
+    return jnp.concatenate(
+        [
+            lat * scale * gain,
+            first * cosine - second * sine,
+            first * sine + second * cosine,
+        ],
+        0,
+    )
+
+
+def project_kernel(order, hid_ref, down_ref, sum_ref, qa_ref, qb_ref, qc_ref):
+    step = pl.program_id(0)
+    rows = hid_ref[...].reshape(LANES, hid_ref.shape[-1])
+    total = lax.dot_general(down_ref[...], rows, NT, preferred_element_type=F32)
+    sum_ref[0] = total
+    for which, ref in enumerate((qa_ref, qb_ref, qc_ref)):
+
+        @pl.when(step == which)
+        def _(ref=ref):
+            encode(total, ref)
+
+
+def project(order, hidden, down_t, unit, units):
+    depth = hidden.shape[-1]
+    coded = jax.ShapeDtypeStruct((CODED, LANES), jnp.int16)
+    whole = pl.BlockSpec((CODED, LANES), lambda i, order: (0, 0))
+    return pl.pallas_call(
+        project_kernel,
+        grid_spec=pltpu.PrefetchScalarGridSpec(
+            num_scalar_prefetch=1,
+            grid=(4,),
+            in_specs=[
+                pl.BlockSpec(
+                    (RP, UNIT, depth), lambda i, order: (0, order[i] * units + unit, 0)
+                ),
+                pl.BlockSpec((WIDTH, depth), lambda i, order: (0, 0)),
+            ],
+            out_specs=[
+                pl.BlockSpec((1, WIDTH, LANES), lambda i, order: (order[i], 0, 0)),
+                whole,
+                whole,
+                whole,
+            ],
+        ),
+        out_shape=[jax.ShapeDtypeStruct((4, WIDTH, LANES), F32), coded, coded, coded],
+        compiler_params=pltpu.CompilerParams(vmem_limit_bytes=40 << 20),
+        cost_estimate=pl.CostEstimate(
+            flops=2 * 4 * LANES * depth * WIDTH,
+            bytes_accessed=4 * LANES * (depth * 2 + WIDTH * 6),
+            transcendentals=0,
+        ),
+        name="project",
+    )(order, hidden, down_t)
+
+
+def add_kernel(where, own_ref, got_ref, pass_ref, out_ref, held_ref):
+    encode(own_ref[0] + decode(got_ref), out_ref)
+
+
+def add_on(where, sums, got, passed):
+    coded = jax.ShapeDtypeStruct((CODED, LANES), jnp.int16)
+    return pl.pallas_call(
+        add_kernel,
+        grid_spec=pltpu.PrefetchScalarGridSpec(
+            num_scalar_prefetch=1,
+            grid=(RP,),
+            in_specs=[
+                pl.BlockSpec((1, WIDTH, UNIT), lambda i, where: (where[0], 0, i)),
+                pl.BlockSpec((CODED, UNIT), lambda i, where: (0, i)),
+                pl.BlockSpec(memory_space=pl.ANY),
+            ],
+            out_specs=[
+                pl.BlockSpec((CODED, UNIT), lambda i, where: (0, i)),
+                pl.BlockSpec(memory_space=pl.ANY),
+            ],
+        ),
+        out_shape=[coded, jax.ShapeDtypeStruct(passed.shape, passed.dtype)],
+        input_output_aliases={3: 1},
+        compiler_params=pltpu.CompilerParams(vmem_limit_bytes=32 << 20),
+        cost_estimate=pl.CostEstimate(
+            flops=8 * LANES * WIDTH, bytes_accessed=8 * LANES * WIDTH, transcendentals=0
+        ),
+        name="add_on",
+    )(where, sums, got, passed)
+
+
+def finish_kernel(where, own_ref, one_ref, two_ref, three_ref, gain_ref, cos_ref, sin_ref, out_ref):
+    comp = own_ref[0] + decode(one_ref) + decode(two_ref) + decode(three_ref)
+    out_ref[...] = key_rows(comp, gain_ref[...], cos_ref[...], sin_ref[...]).astype(BF)
+
+
+def finish(where, sums, blocks, gain, cosine, sine):
+    part = pl.BlockSpec((CODED, UNIT), lambda i, where: (0, i))
+    table = pl.BlockSpec((HALF, UNIT), lambda i, where: (0, 0))
+    return pl.pallas_call(
+        finish_kernel,
+        grid_spec=pltpu.PrefetchScalarGridSpec(
+            num_scalar_prefetch=1,
+            grid=(RP,),
+            in_specs=[
+                pl.BlockSpec((1, WIDTH, UNIT), lambda i, where: (where[0], 0, i)),
+                part,
+                part,
+                part,
+                pl.BlockSpec((KVL, UNIT), lambda i, where: (0, 0)),
+                table,
+                table,
+            ],
+            out_specs=pl.BlockSpec((WIDTH, UNIT), lambda i, where: (0, i)),
+        ),
+        out_shape=jax.ShapeDtypeStruct((WIDTH, LANES), BF),
+        compiler_params=pltpu.CompilerParams(vmem_limit_bytes=32 << 20),
+        cost_estimate=pl.CostEstimate(
+            flops=16 * LANES * WIDTH, bytes_accessed=12 * LANES * WIDTH, transcendentals=0
+        ),
+        name="finish",
+    )(where, sums, *blocks, gain, cosine, sine)
+
+
+def page_kernel(where, slots, has, own_ref, one_ref, two_ref, keys_ref, gain_ref, cos_ref, sin_ref, out_ref):
+    slot = pl.program_id(0)
+    out_ref[...] = jnp.zeros_like(out_ref)
+
+    @pl.when((has[slot] > 0) & (where[0] == 1))
+    def _():
+        comp = own_ref[0] + decode(one_ref) + decode(two_ref)
+        rows = key_rows(comp, gain_ref[...], cos_ref[...], sin_ref[...])
+        out_ref[0] = rows.T.astype(BF)
+
+    @pl.when((has[slot] > 0) & (where[0] != 1))
+    def _():
+        out_ref[0] = keys_ref[...].astype(F32).T.astype(BF)
+
+
+def pages_of(where, slots, has, sums, blocks, keys, gain, cosine, sine):
+    count = slots.shape[0]
+
+    def lane(i, where, slots, has):
+        return (0, slots[i])
+
+    part = pl.BlockSpec((CODED, UNIT), lane)
+    table = pl.BlockSpec((HALF, UNIT), lambda i, *_: (0, 0))
+    return pl.pallas_call(
+        page_kernel,
+        grid_spec=pltpu.PrefetchScalarGridSpec(
+            num_scalar_prefetch=3,
+            grid=(count,),
+            in_specs=[
+                pl.BlockSpec(
+                    (1, WIDTH, UNIT), lambda i, where, slots, has: (where[0], 0, slots[i])
+                ),
+                part,
+                part,
+                pl.BlockSpec((WIDTH, UNIT), lane),
+                pl.BlockSpec((KVL, UNIT), lambda i, *_: (0, 0)),
+                table,
+                table,
+            ],
+            out_specs=pl.BlockSpec((1, UNIT, WIDTH), lambda i, *_: (i, 0, 0)),
+        ),
+        out_shape=jax.ShapeDtypeStruct((count, UNIT, WIDTH), BF),
+        compiler_params=pltpu.CompilerParams(vmem_limit_bytes=32 << 20),
+        cost_estimate=pl.CostEstimate(
+            flops=16 * LANES * WIDTH, bytes_accessed=14 * LANES * WIDTH, transcendentals=0
+        ),
+        name="pages",
+    )(where, slots, has, sums, *blocks, keys, gain, cosine, sine)
+
+
+def query_kernel(lat_ref, up_ref, *refs):
+    *key_refs, cos_ref, sin_ref, out_ref = refs
+    full = jnp.dot(lat_ref[...], up_ref[...], preferred_element_type=F32)
+    for h, key_ref in enumerate(key_refs):
+        base = h * (DN + DR)
+        nope = full[:, base : base + DN].astype(BF)
+        first = full[:, base + DN : base + DN + HALF]
+        second = full[:, base + DN + HALF : base + DN + DR]
+        absorbed = lax.dot_general(nope, key_ref[...], NT, preferred_element_type=F32)
+        cosine, sine = cos_ref[...], sin_ref[...]
+        out_ref[h] = jnp.concatenate(
+            [absorbed, first * cosine - second * sine, first * sine + second * cosine], 1
+        )
+
+
+def queries(latents, q_up, kv_up, cosine, sine):
+    rows = latents.shape[0]
+    heads = q_up.shape[1] // (DN + DR)
+    step = 4
+    key_spec = [
+        pl.BlockSpec((KVL, DN), lambda i, h=h: (0, 2 * (step * i + h))) for h in range(step)
+    ]
+    table = pl.BlockSpec((rows, HALF), lambda i: (0, 0))
+    return pl.pallas_call(
+        query_kernel,
+        grid=(heads // step,),
+        in_specs=[
+            pl.BlockSpec((rows, QL), lambda i: (0, 0)),
+            pl.BlockSpec((QL, step * (DN + DR)), lambda i: (0, i)),
+            *key_spec,
+            table,
+            table,
+        ],
+        out_specs=pl.BlockSpec((step, rows, WIDTH), lambda i: (i, 0, 0)),
+        out_shape=jax.ShapeDtypeStruct((heads, rows, WIDTH), F32),
+        compiler_params=pltpu.CompilerParams(vmem_limit_bytes=32 << 20),
+        cost_estimate=pl.CostEstimate(
+            flops=2 * rows * QL * q_up.shape[1],
+            bytes_accessed=2 * QL * q_up.shape[1] + KVL * kv_up.shape[1],
+            transcendentals=0,
+        ),
+        name="queries",
+    )(latents, q_up, *([kv_up] * step), cosine, sine)
+
+
+def attend_kernel(where, q_ref, *refs):
+    key_refs, (valid_ref, draft_ref), out_refs = refs[:6], refs[6:8], refs[8:]
+    request = pl.program_id(0)
+
+    @pl.when(where[0] == 3)
+    def _():
+        scale = (DN + DR) ** (-0.5)
+        local_rows = q_ref.shape[2]
+        query = q_ref[...].reshape(4 * local_rows, WIDTH)
+        keys = jnp.concatenate([ref[...] for ref in key_refs], 1)
+        drafts = draft_ref[...]
+        scores = jnp.dot(query, keys, preferred_element_type=F32) * scale
+        scores = jnp.where(valid_ref[0] > 0.0, scores, -1e30)
+        fresh = lax.dot_general(query, drafts, NT, preferred_element_type=F32) * scale
+        row = lax.broadcasted_iota(jnp.int32, fresh.shape, 0)
+        late = (row % local_rows) // (local_rows // 2)
+        offset = lax.broadcasted_iota(jnp.int32, fresh.shape, 1) - 2 * request
+        fresh = jnp.where((offset >= 0) & (offset <= late), fresh, -1e30)
+        top = jnp.maximum(
+            jnp.max(scores, axis=1, keepdims=True), jnp.max(fresh, axis=1, keepdims=True)
+        )
+        weights = jnp.exp(scores - top)
+        fresh = jnp.exp(fresh - top)
+        total = jnp.sum(weights, axis=1, keepdims=True) + jnp.sum(fresh, axis=1, keepdims=True)
+        numer = lax.dot_general(weights.astype(BF), keys[:KVL], NT, preferred_element_type=F32)
+        numer = numer + jnp.dot(fresh.astype(BF), drafts[:, :KVL], preferred_element_type=F32)
+        result = (numer / total).astype(BF)
+        for t, ref in enumerate(out_refs):
+            ref[0] = result[t * local_rows : (t + 1) * local_rows]
+
+
+def attend(where, query, keys, valid, drafts):
+    local_rows = query.shape[2]
+    key_spec = pl.BlockSpec((WIDTH, UNIT), lambda i, where: (0, i))
+    out = jax.ShapeDtypeStruct((RP, local_rows, KVL), BF)
+    return pl.pallas_call(
+        attend_kernel,
+        grid_spec=pltpu.PrefetchScalarGridSpec(
+            num_scalar_prefetch=1,
+            grid=(RP,),
+            in_specs=[
+                pl.BlockSpec((4, 1, local_rows, WIDTH), lambda i, where: (0, i, 0, 0)),
+                *([key_spec] * len(keys)),
+                pl.BlockSpec((1, 1, valid.shape[2]), lambda i, where: (i, 0, 0)),
+                pl.BlockSpec(drafts.shape, lambda i, where: (0, 0)),
+            ],
+            out_specs=[pl.BlockSpec((1, local_rows, KVL), lambda i, where: (i, 0, 0))] * 4,
+        ),
+        out_shape=[out] * 4,
+        compiler_params=pltpu.CompilerParams(vmem_limit_bytes=40 << 20),
+        cost_estimate=pl.CostEstimate(
+            flops=2 * RP * 4 * local_rows * 768 * (WIDTH + KVL),
+            bytes_accessed=8 << 20,
+            transcendentals=RP * 4 * local_rows * 768,
+        ),
+        name="attend",
+    )(where, query, *keys, valid, drafts)
+
+
+def heads_kernel(o_ref, keep_ref, *refs):
+    *value_refs, out_ref = refs
+    for h, value_ref in enumerate(value_refs):
+        row = jnp.dot(o_ref[h].astype(BF), value_ref[...], preferred_element_type=F32)
+        out_ref[:, h * DV : (h + 1) * DV] = row * keep_ref[...]
+
+
+def heads_out(attended, keep, kv_up):
+    heads, rows, _ = attended.shape
+    step = 8
+    value_spec = [
+        pl.BlockSpec((KVL, DV), lambda i, h=h: (0, 2 * (step * i + h) + 1)) for h in range(step)
+    ]
+    return pl.pallas_call(
+        heads_kernel,
+        grid=(heads // step,),
+        in_specs=[
+            pl.BlockSpec((step, rows, KVL), lambda i: (i, 0, 0)),
+            pl.BlockSpec((rows, DV), lambda i: (0, 0)),
+            *value_spec,
+        ],
+        out_specs=pl.BlockSpec((rows, step * DV), lambda i: (0, i)),
+        out_shape=jax.ShapeDtypeStruct((rows, heads * DV), F32),
+        compiler_params=pltpu.CompilerParams(vmem_limit_bytes=32 << 20),
+        cost_estimate=pl.CostEstimate(
+            flops=2 * rows * KVL * heads * DV, bytes_accessed=KVL * heads * DV * 2, transcendentals=0
+        ),
+        name="heads_out",
+    )(attended, keep, *([kv_up] * step))
+
+
+def rope_tables(position):
+    freq = jnp.exp(-jnp.log(10000.0) * jnp.arange(HALF, dtype=F32) / HALF)
+    angle = position.astype(F32)[..., None] * freq
+    return jnp.cos(angle), jnp.sin(angle)
+
+
+def local_line(
+    prefill_hidden,
+    draft_hidden,
+    kv_down,
+    kv_gain,
+    query_latent,
+    q_up,
+    kv_up,
+    owners,
+    segment_ids,
+    accepted,
+):
+    pd_count = lax.axis_size("pd")
+    z = lax.axis_index("tp")
+    p = lax.axis_index("pd")
+    share = PRE_TOK // 4
+    units = share // UNIT
+    first_req = p * RP
+    where = z.astype(jnp.int32).reshape(1)
+
+    def pick(*choices):
+        return jnp.asarray(choices, jnp.int32)[z].reshape(1)
+
+    order = jnp.asarray([[3, 2, 1, 0], [3, 2, 0, 1], [3, 2, 0, 1], [0, 2, 1, 3]], jnp.int32)[z]
+    hidden = prefill_hidden.reshape(RP, PRE_TOK, prefill_hidden.shape[1])
+    down_t = kv_down.T
+    work = [project(order, hidden, down_t, u, units) for u in range(units)]
+    sums = [w[0] for w in work]
+    coded = [list(w[1:]) for w in work]
+
+    latents = lax.dynamic_slice_in_dim(query_latent, first_req, RP, 0).reshape(RP * 2, QL)
+    new_pos = jnp.tile(PRE_TOK + jnp.arange(2, dtype=jnp.int32), RP)
+    new_cos, new_sin = rope_tables(new_pos)
+    query = queries(latents, q_up, kv_up, new_cos, new_sin)
+    heads = query.shape[0]
+    query = (
+        query.reshape(heads, RP, 2, WIDTH).transpose(1, 2, 0, 3).reshape(RP, 2 * heads, WIDTH)
+    ).astype(BF)
+    query = lax.all_gather(query, "tp", axis=0)
+    draft = jnp.dot(draft_hidden, kv_down, preferred_element_type=F32)
+    draft = jnp.sum(lax.all_gather(draft, "tp", axis=0), axis=0)
+    draft_keys = jnp.concatenate(
+        [rms_latent(draft, kv_gain), rotate(draft[:, KVL:], new_pos).astype(BF)], 1
+    )
+    draft_keys = jnp.pad(draft_keys, ((0, UNIT - RP * 2), (0, 0)))
+    my_segments = lax.dynamic_slice_in_dim(segment_ids, first_req, RP, 0)
+    valid = (my_segments == my_segments[:, -1:])[:, PRE_TOK // 2 :].astype(F32)
+    valid = valid.reshape(RP, 1, PRE_TOK // 2)
+
+    gain = jnp.broadcast_to(kv_gain[:, None], (KVL, UNIT))
+    position = z * share + jnp.arange(share, dtype=jnp.int32).reshape(units, UNIT)
+    cosine, sine = rope_tables(position)
+    cosine, sine = jnp.swapaxes(cosine, 1, 2), jnp.swapaxes(sine, 1, 2)
+
+    inward = [(0, 1), (3, 2)]
+    sends = [(u, k) for u in range(units) for k in (0, 1)] + [(u, 2) for u in range(units)]
+    own_of_add = {0: pick(0, 3, 0, 0), 1: pick(0, 2, 0, 0), 2: pick(0, 0, 1, 0)}
+    got = {}
+    added = {}
+    nothing = jnp.zeros((8, 128), jnp.int16)
+    for at, (u, k) in enumerate(sends):
+        got[u, k] = lax.ppermute(coded[u][k], "tp", inward)
+        ahead = sends[at + 2] if at + 2 < len(sends) else None
+        passed = nothing if ahead is None else coded[ahead[0]][ahead[1]]
+        added[u, k], passed = add_on(own_of_add[k], sums[u], got[u, k], passed)
+        if ahead is not None:
+            coded[ahead[0]][ahead[1]] = passed
+
+    early = []
+    moved = []
+    own_mid = pick(0, 0, 3, 0)
+    for u in range(units):
+        outer = lax.ppermute(added[u, 0], "tp", [(1, 2), (2, 1)])
+        outer, _ = add_on(own_mid, sums[u], outer, nothing)
+        outer = lax.ppermute(outer, "tp", [(2, 3), (1, 0)])
+        middle = lax.ppermute(added[u, 1], "tp", [(1, 2)])
+        keys = finish(where, sums[u], (outer, got[u, 1], middle), gain, cosine[u], sine[u])
+        early.append(keys)
+        moved.append(lax.ppermute(keys, "tp", [(2, 3)]))
+
+    result = attend(where, query, moved + early, valid, draft_keys)
+    back = [lax.ppermute(result[t], "tp", [(3, t)]) for t in range(3)]
+    attended = jnp.where(z == 3, result[3], back[0] + back[1] + back[2])
+    attended = attended.reshape(RP, 2, heads, KVL).transpose(2, 0, 1, 3)
+    attended = attended.reshape(heads, RP * 2, KVL).astype(F32)
+    my_accepted = lax.dynamic_slice_in_dim(accepted, first_req, RP, 0)
+    keep = (jnp.arange(2)[None, :] <= my_accepted[:, None]).astype(F32).reshape(RP * 2, 1)
+    answer = heads_out(attended, jnp.broadcast_to(keep, (RP * 2, DV)), kv_up)
+    answer = answer.reshape(RP, 2, heads * DV)
+
+    my_owners = lax.dynamic_slice_in_dim(owners, first_req, RP, 0)
+    routing = my_owners[None, :] == jnp.arange(pd_count, dtype=jnp.int32)[:, None]
+    has = jnp.any(routing, axis=1)
+    slots = jnp.sum(routing.astype(jnp.int32) * jnp.arange(RP, dtype=jnp.int32)[None, :], axis=1)
+    placed = jnp.where(has[:, None, None], answer[slots], 0.0).astype(BF)
+    placed = lax.all_to_all(placed, "pd", split_axis=0, concat_axis=0, tiled=True)
+
+    pages = []
+    for u in range(units):
+        last = lax.ppermute(added[u, 2], "tp", [(2, 1)])
+        page = pages_of(
+            where,
+            slots,
+            has.astype(jnp.int32),
+            sums[u],
+            (got[u, 2], last),
+            early[u],
+            gain,
+            cosine[u],
+            sine[u],
+        )
+        pages.append(lax.all_to_all(page, "pd", split_axis=0, concat_axis=0, tiled=True))
+    return (placed.reshape(pd_count * 2, heads * DV), jnp.concatenate(pages, 1))
+
+
 def solution(mesh):
     placed = (
         P(("groups", "pd"), "tp"),
@@ -191,7 +656,7 @@
         P("groups"),
     )
     return jax.shard_map(
-        local,
+        local_line if mesh.shape["tp"] == 4 else local_general,
         mesh=mesh,
         in_specs=placed,
         out_specs=(P(("groups", "pd"), "tp"), P(("groups", "pd"), "tp", None)),

time: 570 us -> 324 us (0.57)
  waiting for transfers between devices: 328 us -> 63.2 us
  Pallas kernels: 0 us -> 92.8 us
  local copies, waits for them, and re-layouts: 109 us -> 47 us
  starting transfers between devices: 8.04 us -> 68.6 us
  matrix products: 55.2 us -> 0.63 us
  loops' own time: 14.5 us -> 0 us
  other arithmetic: 18.6 us -> 6.44 us
  blocking collectives: 18.3 us -> 27.9 us
    reduce_scatter x1 -> x0, waiting for transfers between devices: 181 us -> none  [local(): lax.psum_scatter(jnp.einsum('rtd,dw->trw', local_hidden, kv_down, preferr...]
    all_gather x4 -> x1, waiting for transfers between devices: 146 us -> 0.02 us  [local_line(): query = lax.all_gather(query, 'tp', axis=0)]
    pallas_call x0 -> x24, Pallas kernels: none -> 92.8 us  [the longest x12 29.5 us: add_on(): pl.pallas_call(add_kernel, grid_spec=pltpu.PrefetchScalarGridSpec(num_sca...]
    dot_general x34 -> x1, matrix products: 55.2 us -> 0.63 us  [local_line(): draft = jnp.dot(draft_hidden, kv_down, preferred_element_type=F32)]
    ppermute x0 -> x27, starting transfers between devices: none -> 53.3 us  [the longest x3 12.6 us: local_line(): moved.append(lax.ppermute(keys, 'tp', [(2, 3)]))]
    ppermute x0 -> x27, waiting for transfers between devices: none -> 45.5 us  [the longest x9 13.3 us: local_line(): got[u, k] = lax.ppermute(coded[u][k], 'tp', inward)]
    all_gather x0 -> x1, blocking collectives: none -> 27.9 us  [local_line(): draft = jnp.sum(lax.all_gather(draft, 'tp', axis=0), axis=0)]
    reshape x6 -> x4, local copies, waits for them, and re-layouts: 28 us -> 0.74 us  [the longest x1 0.66 us: local_line(): return (placed.reshape(pd_count * 2, heads * DV), jnp.concatenate(pages, 1))]
  transfers between devices with their start and end apart: 7 -> 32, of which waited for: 5 -> 10; matrix products, arithmetic and copies ran while one was open for 19% -> 4% of each run, Pallas kernels for 0% -> 26%
where the time goes in v1:
time: 324 us; the launch traced here: 321 us
  Pallas kernels  92.8 us (29%)
  starting transfers between devices  68.6 us (21%)
  waiting for transfers between devices  63.2 us (20%)
  local copies, waits for them, and re-layouts  47 us (15%)
  blocking collectives  27.9 us (9%)
  between operations  15 us (5%)
  other arithmetic  6.44 us (2%)
    unnamed x94, local copies, waits for them, and re-layouts  36.3 us
    pallas_call x12, Pallas kernels, add_on(): pl.pallas_call(add_kernel, grid_spec=pltpu.PrefetchScalarGridSpec(num_sca...  29.5 us
    all_gather x1, blocking collectives, local_line(): draft = jnp.sum(lax.all_gather(draft, 'tp', axis=0), axis=0)  27.9 us
    pallas_call x3, Pallas kernels, project(): pl.pallas_call(project_kernel, grid_spec=pltpu.PrefetchScalarGridSpec(num...  26.3 us
    all_to_all x3, waiting for transfers between devices, local_line(): lax.all_to_all(page, 'pd', split_axis=0, concat_axis=0, tiled=True)  17.7 us
    ppermute x9, waiting for transfers between devices, local_line(): got[u, k] = lax.ppermute(coded[u][k], 'tp', inward)  13.3 us
    ppermute x3, waiting for transfers between devices, local_line(): outer = lax.ppermute(outer, 'tp', [(2, 3), (1, 0)])  13.1 us
    ppermute x3, waiting for transfers between devices, local_line(): moved.append(lax.ppermute(keys, 'tp', [(2, 3)]))  13 us
  transfers between devices with their start and end apart: 32, of which 10 were waited for; matrix products, arithmetic and copies ran while one was open for 4% of the time, Pallas kernels for 26%

profile of v1, /device:TPU:16, one launch (start us, length us, event | category | flops | bytes accessed | tf_op | source)
XLA Modules:
  0.0 321.5 jit_solution(15611281291404759079)
XLA Ops:
  9.5 8.1 %project.3 = (f32[4,576,512]{2,1,0:T(8,128)S(1)}, s16[592,512]{1,0:T(8,128)(2,1)S(1)}, s16[592,512]{1,0:T(8,128)(2,1)S(1)}, s16[592,512]{1,0:T(8,128)(2,1)S(1)}) custom-call(s32[4]{0:T(128)S(1)} %dynamic-slice_bitcast_fusion.order, bf16[4,1536,1792]{2,1,0:T(8,128)(2,1)} %bitcast.41, bf16[576,1792]{1,0:T(8,128)(2,1)S(1)} %bitcast.38), custom_call_target="tpu_custom_call" | custom-call | flops 4227858432 | bytes 14417920 | tf_op jit(solution)/shard_map/project/pallas_call | solution.py:246
  20.9 8.9 %project.4 = (f32[4,576,512]{2,1,0:T(8,128)S(1)}, s16[592,512]{1,0:T(8,128)(2,1)S(1)}, s16[592,512]{1,0:T(8,128)(2,1)}, s16[592,512]{1,0:T(8,128)(2,1)S(1)}) custom-call(s32[4]{0:T(128)S(1)} %dynamic-slice_bitcast_fusion.order, bf16[4,1536,1792]{2,1,0:T(8,128)(2,1)} %bitcast.42, bf16[576,1792]{1,0:T(8,128)(2,1)S(1)} %bitcast.39), custom_call_target="tpu_custom_call" | custom-call | flops 4227858432 | bytes 14417920 | tf_op jit(solution)/shard_map/project/pallas_call | solution.py:246
  29.8 6.3 %collective-permute-done.got_ref = s16[592,512]{1,0:T(8,128)(2,1)S(1)} collective-permute-done((s16[592,512]{1,0:T(8,128)(2,1)S(1)}, s16[592,512]{1,0:T(8,128)(2,1)S(1)}, u32[]{:S(2)}, u32[]{:S(2)}) %collective-permute-start) | collective-permute-done | bytes 606240 | tf_op jit(solution)/shard_map/ppermute | solution.py:591
  36.1 2.6 add_on.12
  40.6 9.2 %project.5 = (f32[4,576,512]{2,1,0:T(8,128)S(1)}, s16[592,512]{1,0:T(8,128)(2,1)}, s16[592,512]{1,0:T(8,128)(2,1)S(1)}, s16[592,512]{1,0:T(8,128)(2,1)}) custom-call(s32[4]{0:T(128)S(1)} %dynamic-slice_bitcast_fusion.order, bf16[4,1536,1792]{2,1,0:T(8,128)(2,1)} %bitcast.43, bf16[576,1792]{1,0:T(8,128)(2,1)S(1)} %bitcast.40), custom_call_target="tpu_custom_call" | custom-call | flops 4227858432 | bytes 14417920 | tf_op jit(solution)/shard_map/project/pallas_call | solution.py:246
  49.8 2.3 collective-permute-start.1
  55.1 7.0 %collective-permute-done.6.got_ref = s16[592,512]{1,0:T(8,128)(2,1)S(1)} collective-permute-done((s16[592,512]{1,0:T(8,128)(2,1)S(1)}, s16[592,512]{1,0:T(8,128)(2,1)S(1)}, u32[]{:S(2)}, u32[]{:S(2)}) %collective-permute-start.6) | collective-permute-done | bytes 606240 | tf_op jit(solution)/shard_map/ppermute | solution.py:591
  62.1 2.6 add_on.15
  66.6 27.9 %all-gather = f32[32,576]{1,0:T(8,128)S(1)} all-gather(f32[8,576]{1,0:T(8,128)S(1)} %fusion.9), channel_id=2, replica_groups=mesh['groups'=2,'tp'=4,'pd'=4] {'tp'}, dimensions={0}, use_global_device_ids=true | all-gather | bytes 92160 | tf_op jit(solution)/shard_map/all_gather | solution.py:570
  94.6 2.3 copy-done.10
  105.0 2.3 copy-done.5
  107.3 4.2 %add_on.18 = (s16[592,512]{1,0:T(8,128)(2,1)}, s16[592,512]{1,0:T(8,128)(2,1)S(1)}) custom-call(s32[1]{0:T(128)} %dynamic_slice.31.where, f32[4,576,512]{2,1,0:T(8,128)S(1)} %copy-done.5, s16[592,512]{1,0:T(8,128)(2,1)} %collective-permute-done.12.got_ref, s16[592,512]{1,0:T(8,128)(2,1)S(1)} %get-tuple-element.55.pass_ref), custom_call_target="tpu_custom_call", output_to_operand_aliasing={{1}: (3, {})} | custom-call | flops 2359296 | bytes 2359296 | tf_op jit(solution)/shard_map/add_on/pallas_call | solution.py:281
  113.6 5.4 %collective-permute-start.13 = (s16[592,512]{1,0:T(8,128)(2,1)}, s16[592,512]{1,0:T(8,128)(2,1)}, u32[]{:S(2)}, u32[]{:S(2)}) collective-permute-start(s16[592,512]{1,0:T(8,128)(2,1)} %get-tuple-element.56), channel_id=1, source_target_pairs={{4,8},{8,4},{5,9},{9,5},{6,10},{10,6},{7,11},{11,7},{20,24},{24,20... | collective-permute-start | bytes 1818632 | tf_op jit(solution)/shard_map/ppermute | solution.py:602
  119.2 3.4 %copy-done.2 = bf16[512,8192]{1,0:T(8,128)(2,1)S(1)} copy-done((bf16[512,8192]{1,0:T(8,128)(2,1)S(1)}, bf16[512,8192]{1,0:T(8,128)(2,1)}, u32[]{:S(2)}) %copy-start.2) | copy-done | bytes 8388632
  122.6 11.0 %queries.1 = f32[32,8,576]{2,1,0:T(8,128)S(1)} custom-call(bf16[8,1536]{1,0:T(8,128)(2,1)S(1)} %reshape.126.lat_ref, bf16[1536,6144]{1,0:T(8,128)(2,1)} %up_ref.1, bf16[512,8192]{1,0:T(8,128)(2,1)S(1)} %copy-done.2, bf16[512,8192]{1,0:T(8,128)(2,1)S(1)} %copy-done.2, bf16[512,8192]{1,0:T(8,128)(2,1)S(1)} %copy-done.2, bf16[512,8192]{1,0:T(8,128)(2,1)S(1)} %copy-done.2, ...), custom_call_target="tpu_custom_call" | custom-call | flops 150994944 | bytes 23068672 | tf_op jit(solution)/shard_map/queries/pallas_call | solution.py:412
  137.1 2.3 copy-done.14
  140.5 2.6 add_on.13
  146.5 2.4 copy-done.6
  152.4 2.4 copy-done.11
  154.8 3.1 add_on.16
  159.3 3.7 %add_on.19 = (s16[592,512]{1,0:T(8,128)(2,1)S(1)}, s16[8,128]{1,0:T(8,128)(2,1)S(1)}) custom-call(s32[1]{0:T(128)} %dynamic_slice.30.where, f32[4,576,512]{2,1,0:T(8,128)S(1)} %bitcast.33, s16[592,512]{1,0:T(8,128)(2,1)} %collective-permute-done.13.got_ref, s16[8,128]{1,0:T(8,128)(2,1)S(1)} %broadcast_in_dim.15.clone.2.pass_ref), custom_call_target="tpu_custom_call", output_to_operand_aliasing={{1}: (3, {})} | custom-call | flops 2359296 | bytes 2359296 | tf_op jit(solution)/shard_map/add_on/pallas_call | solution.py:281
  170.8 7.0 %collective-permute-done.2.one_ref = s16[592,512]{1,0:T(8,128)(2,1)} collective-permute-done((s16[592,512]{1,0:T(8,128)(2,1)}, s16[592,512]{1,0:T(8,128)(2,1)}, u32[]{:S(2)}, u32[]{:S(2)}) %collective-permute-start.2) | collective-permute-done | bytes 606240 | tf_op jit(solution)/shard_map/ppermute | solution.py:604
  179.1 3.0 collective-permute-start.22
  182.5 3.9 %finish.3.refs_3_.keys_ref = bf16[576,512]{1,0:T(8,128)(2,1)} custom-call(s32[1]{0:T(128)} %bitcast.where, f32[4,576,512]{2,1,0:T(8,128)S(1)} %copy-done.15, s16[592,512]{1,0:T(8,128)(2,1)} %collective-permute-done.2.one_ref, s16[592,512]{1,0:T(8,128)(2,1)S(1)} %collective-permute-done.3.got_ref.two_ref, s16[592,512]{1,0:T(8,128)(2,1)} %collective-permute-done.4.three_ref, ...), custom_call_target="tpu_custom_call" | custom-call | flops 4718592 | bytes 3538944 | tf_op jit(solution)/shard_map/finish/pallas_call | solution.py:314
  186.4 4.3 %collective-permute-done.8.one_ref = s16[592,512]{1,0:T(8,128)(2,1)S(1)} collective-permute-done((s16[592,512]{1,0:T(8,128)(2,1)S(1)}, s16[592,512]{1,0:T(8,128)(2,1)S(1)}, u32[]{:S(2)}, u32[]{:S(2)}) %collective-permute-start.8) | collective-permute-done | bytes 606240 | tf_op jit(solution)/shard_map/ppermute | solution.py:604
  190.7 5.2 %collective-permute-start.5 = (bf16[576,512]{1,0:T(8,128)(2,1)}, bf16[576,512]{1,0:T(8,128)(2,1)}, u32[]{:S(2)}, u32[]{:S(2)}) collective-permute-start(bf16[576,512]{1,0:T(8,128)(2,1)} %finish.3.refs_3_.keys_ref), channel_id=1, source_target_pairs={{8,12},{9,13},{10,14},{11,15},{24,28},{25,29},{26,30},{27,31}} | collective-permute-start | bytes 1769480 | tf_op jit(solution)/shard_map/ppermute | solution.py:608
  195.9 3.8 %finish.4.refs_4_.keys_ref = bf16[576,512]{1,0:T(8,128)(2,1)} custom-call(s32[1]{0:T(128)} %bitcast.where, f32[4,576,512]{2,1,0:T(8,128)S(1)} %bitcast.35, s16[592,512]{1,0:T(8,128)(2,1)S(1)} %collective-permute-done.8.one_ref, s16[592,512]{1,0:T(8,128)(2,1)S(1)} %collective-permute-done.9.got_ref.two_ref, ...), custom_call_target="tpu_custom_call" | custom-call | flops 4718592 | bytes 3538944 | tf_op jit(solution)/shard_map/finish/pallas_call | solution.py:314
  203.7 2.4 finish.5.refs_5_.keys_ref
  206.1 5.2 %collective-permute-start.17 = (bf16[576,512]{1,0:T(8,128)(2,1)}, bf16[576,512]{1,0:T(8,128)(2,1)}, u32[]{:S(2)}, u32[]{:S(2)}) collective-permute-start(bf16[576,512]{1,0:T(8,128)(2,1)} %finish.5.refs_5_.keys_ref), channel_id=1, source_target_pairs={{8,12},{9,13},{10,14},{11,15},{24,28},{25,29},{26,30},{27,31}} | collective-permute-start | bytes 1769480 | tf_op jit(solution)/shard_map/ppermute | solution.py:608
  211.5 2.7 add_on.22
  217.8 3.3 %pages.3 = bf16[4,128,576]{2,1,0:T(8,128)(2,1)S(1)} custom-call(s32[1]{0:T(128)} %bitcast.where, s32[4]{0:T(128)S(1)} %select_reduce_fusion.slots, s32[4]{0:T(128)S(1)} %convert_element_type.108.has, f32[4,576,512]{2,1,0:T(8,128)S(1)} %bitcast.37, s16[592,512]{1,0:T(8,128)(2,1)S(1)} %collective-permute-done.21.got_ref.one_ref, ...), custom_call_target="tpu_custom_call" | custom-call | flops 4718592 | bytes 4128768 | tf_op jit(solution)/shard_map/pages/pallas_call | solution.py:362
  222.1 4.3 %all-to-all-start.1 = ((bf16[4,128,576]{1,2,0:T(8,128)(2,1)}), bf16[4,128,576]{1,2,0:T(8,128)(2,1)}, u32[]{:S(2)}, u32[]{:S(2)}) async-start(bf16[4,128,576]{1,2,0:T(8,128)(2,1)} %copy.42), calls=%async_computation.1 | async-start | bytes 1179648 | tf_op jit(solution)/shard_map/all_to_all | solution.py:641
  226.4 2.6 collective-permute-done.11.refs_1_
  229.1 10.3 %collective-permute-done.17.refs_2_ = bf16[576,512]{1,0:T(8,128)(2,1)} collective-permute-done((bf16[576,512]{1,0:T(8,128)(2,1)}, bf16[576,512]{1,0:T(8,128)(2,1)}, u32[]{:S(2)}, u32[]{:S(2)}) %collective-permute-start.17) | collective-permute-done | bytes 589856 | tf_op jit(solution)/shard_map/ppermute | solution.py:608
  240.7 3.8 %attend.1 = (bf16[4,64,512]{2,1,0:T(8,128)(2,1)}, bf16[4,64,512]{2,1,0:T(8,128)(2,1)S(1)}, bf16[4,64,512]{2,1,0:T(8,128)(2,1)S(1)}, bf16[4,64,512]{2,1,0:T(8,128)(2,1)S(1)}) custom-call(s32[1]{0:T(128)} %bitcast.where, bf16[4,4,64,576]{3,2,1,0:T(8,128)(2,1)S(1)} %copy-done.27, bf16[576,512]{1,0:T(8,128)(2,1)} %collective-permute-done.5.refs_0_, ...), custom_call_target="tpu_custom_call" | custom-call | flops 1711276032 | bytes 8388608 | tf_op jit(solution)/shard_map/attend/pallas_call | solution.py:469
  251.0 3.4 %pages.4 = bf16[4,128,576]{2,1,0:T(8,128)(2,1)S(1)} custom-call(s32[1]{0:T(128)} %bitcast.where, s32[4]{0:T(128)S(1)} %select_reduce_fusion.slots, s32[4]{0:T(128)S(1)} %convert_element_type.108.has, f32[4,576,512]{2,1,0:T(8,128)S(1)} %copy-done.12, s16[592,512]{1,0:T(8,128)(2,1)S(1)} %copy-done.18, s16[592,512]{1,0:T(8,128)(2,1)} %collective-permute-done.24.two_ref, ...), custom_call_target="tpu_custom_call" | custom-call | flops 4718592 | bytes 4128768 | tf_op jit(solution)/shard_map/pages/pallas_call | solution.py:362
  255.5 2.3 copy-done.7
  260.8 6.0 %collective-permute-done.20 = bf16[4,64,512]{2,1,0:T(8,128)(2,1)} collective-permute-done((bf16[4,64,512]{2,1,0:T(8,128)(2,1)S(1)}, bf16[4,64,512]{2,1,0:T(8,128)(2,1)}, u32[]{:S(2)}, u32[]{:S(2)}) %collective-permute-start.20) | collective-permute-done | bytes 262176 | tf_op jit(solution)/shard_map/ppermute | solution.py:611
  268.7 3.4 %copy-done.3 = bf16[512,8192]{1,0:T(8,128)(2,1)S(1)} copy-done((bf16[512,8192]{1,0:T(8,128)(2,1)S(1)}, bf16[512,8192]{1,0:T(8,128)(2,1)}, u32[]{:S(2)}) %copy-start.3) | copy-done | bytes 8388632
  272.1 2.3 heads_out.1
  275.2 4.2 %all-to-all-start.2 = ((bf16[4,128,576]{1,2,0:T(8,128)(2,1)}), bf16[4,128,576]{1,2,0:T(8,128)(2,1)}, u32[]{:S(2)}, u32[]{:S(2)}) async-start(bf16[4,128,576]{1,2,0:T(8,128)(2,1)} %copy.43), calls=%async_computation.2 | async-start | bytes 1179648 | tf_op jit(solution)/shard_map/all_to_all | solution.py:641
  280.1 8.9 %all-to-all-done.2 = bf16[4,128,576]{1,2,0:T(8,128)(2,1)} async-done(((bf16[4,128,576]{1,2,0:T(8,128)(2,1)}), bf16[4,128,576]{1,2,0:T(8,128)(2,1)}, u32[]{:S(2)}, u32[]{:S(2)}) %all-to-all-start.2) | async-done | bytes 589856 | tf_op jit(solution)/shard_map/all_to_all | solution.py:641
  289.0 3.3 %all-to-all-start = ((bf16[4,2,4096]{2,1,0:T(2,128)(2,1)}), bf16[4,2,4096]{2,1,0:T(2,128)(2,1)S(1)}, u32[]{:S(2)}, u32[]{:S(2)}) async-start(bf16[4,2,4096]{2,1,0:T(2,128)(2,1)} %select_convert_fusion), calls=%async_computation | async-start | bytes 131072 | tf_op jit(solution)/shard_map/all_to_all | solution.py:625
  292.3 2.3 copy-done.8
  294.6 3.3 %pages.5 = bf16[4,128,576]{2,1,0:T(8,128)(2,1)S(1)} custom-call(s32[1]{0:T(128)} %bitcast.where, s32[4]{0:T(128)S(1)} %select_reduce_fusion.slots, s32[4]{0:T(128)S(1)} %convert_element_type.108.has, f32[4,576,512]{2,1,0:T(8,128)S(1)} %copy-done.8, s16[592,512]{1,0:T(8,128)(2,1)S(1)} %collective-permute-done.25.got_ref.one_ref, ...), custom_call_target="tpu_custom_call" | custom-call | flops 4718592 | bytes 4128768 | tf_op jit(solution)/shard_map/pages/pallas_call | solution.py:362
  298.9 3.5 %all-to-all-start.3 = ((bf16[4,128,576]{1,2,0:T(8,128)(2,1)}), bf16[4,128,576]{1,2,0:T(8,128)(2,1)S(1)}, u32[]{:S(2)}, u32[]{:S(2)}) async-start(bf16[4,128,576]{1,2,0:T(8,128)(2,1)} %copy.44), calls=%async_computation.3 | async-start | bytes 1179648 | tf_op jit(solution)/shard_map/all_to_all | solution.py:641
  303.1 8.9 %all-to-all-done.3 = bf16[4,128,576]{1,2,0:T(8,128)(2,1)S(1)} async-done(((bf16[4,128,576]{1,2,0:T(8,128)(2,1)}), bf16[4,128,576]{1,2,0:T(8,128)(2,1)S(1)}, u32[]{:S(2)}, u32[]{:S(2)}) %all-to-all-start.3) | async-done | bytes 589856 | tf_op jit(solution)/shard_map/all_to_all | solution.py:641
  311.9 2.7 pad_maximum_fusion
  (193 shorter events, 70.3 us)
Async XLA Ops:
  7.2 87.4 %copy-start = (bf16[16,2,1536]{2,1,0:T(2,128)(2,1)S(1)}, bf16[16,2,1536]{2,1,0:T(2,128)(2,1)}, u32[]{:S(2)}) copy-start(bf16[16,2,1536]{2,1,0:T(2,128)(2,1)} %param.19) | copy-start | bytes 294916
  7.2 219.2 %all-gather.3.cloned.1.call-start = ((), (), s32[]{:S(2)}) async-start(), calls=%async_computation.4 | async-start | bytes 1638400 | tf_op jit(solution)/shard_map/all_gather | solution.py:568
  17.7 34.5 %copy-start.13 = (f32[4,576,512]{2,1,0:T(8,128)}, f32[4,576,512]{2,1,0:T(8,128)S(1)}, u32[]{:S(2)}) copy-start(f32[4,576,512]{2,1,0:T(8,128)S(1)} %get-tuple-element.37.own_ref) | copy-start | bytes 14155780
  17.7 18.5 %collective-permute-start = (s16[592,512]{1,0:T(8,128)(2,1)S(1)}, s16[592,512]{1,0:T(8,128)(2,1)S(1)}, u32[]{:S(2)}, u32[]{:S(2)}) collective-permute-start(s16[592,512]{1,0:T(8,128)(2,1)S(1)} %get-tuple-element.38), channel_id=1, source_target_pairs={{0,4},{12,8},{1,5},{13,9},{2,6},{14,10},{3,7},{15,11},{16,20},{28,... | collective-permute-start | bytes 1818632 | tf_op jit(solution)/shard_map/ppermute | solution.py:591
  19.0 33.2 %collective-permute-start.3 = (s16[592,512]{1,0:T(8,128)(2,1)S(1)}, s16[592,512]{1,0:T(8,128)(2,1)S(1)}, u32[]{:S(2)}, u32[]{:S(2)}) collective-permute-start(s16[592,512]{1,0:T(8,128)(2,1)S(1)} %get-tuple-element.42), channel_id=1, source_target_pairs={{0,4},{12,8},{1,5},{13,9},{2,6},{14,10},{3,7},{15,11},{16,20},{28,... | collective-permute-start | bytes 1818632 | tf_op jit(solution)/shard_map/ppermute | solution.py:591
  29.8 32.3 %copy-start.9 = (f32[4,576,512]{2,1,0:T(8,128)}, f32[4,576,512]{2,1,0:T(8,128)S(1)}, u32[]{:S(2)}) copy-start(f32[4,576,512]{2,1,0:T(8,128)S(1)} %get-tuple-element.45.own_ref) | copy-start | bytes 14155780
  38.7 23.4 %collective-permute-start.6 = (s16[592,512]{1,0:T(8,128)(2,1)S(1)}, s16[592,512]{1,0:T(8,128)(2,1)S(1)}, u32[]{:S(2)}, u32[]{:S(2)}) collective-permute-start(s16[592,512]{1,0:T(8,128)(2,1)S(1)} %get-tuple-element.46), channel_id=1, source_target_pairs={{0,4},{12,8},{1,5},{13,9},{2,6},{14,10},{3,7},{15,11},{16,20},{28,... | collective-permute-start | bytes 1818632 | tf_op jit(solution)/shard_map/ppermute | solution.py:591
  49.8 14.9 %copy-start.4 = (f32[4,576,512]{2,1,0:T(8,128)}, f32[4,576,512]{2,1,0:T(8,128)S(1)}, u32[]{:S(2)}) copy-start(f32[4,576,512]{2,1,0:T(8,128)S(1)} %get-tuple-element.53.own_ref) | copy-start | bytes 14155780
  49.8 63.8 %collective-permute-start.1 = (s16[592,512]{1,0:T(8,128)(2,1)}, s16[592,512]{1,0:T(8,128)(2,1)S(1)}, u32[]{:S(2)}, u32[]{:S(2)}) collective-permute-start(s16[592,512]{1,0:T(8,128)(2,1)} %get-tuple-element.40), channel_id=1, source_target_pairs={{4,8},{8,4},{5,9},{9,5},{6,10},{10,6},{7,11},{11,7},{20,24},{24,20... | collective-permute-start | bytes 1818632 | tf_op jit(solution)/shard_map/ppermute | solution.py:602
  53.7 40.9 %collective-permute-start.9 = (s16[592,512]{1,0:T(8,128)(2,1)}, s16[592,512]{1,0:T(8,128)(2,1)S(1)}, u32[]{:S(2)}, u32[]{:S(2)}) collective-permute-start(s16[592,512]{1,0:T(8,128)(2,1)} %get-tuple-element.50), channel_id=1, source_target_pairs={{0,4},{12,8},{1,5},{13,9},{2,6},{14,10},{3,7},{15,11},{16,20},{28,... | collective-permute-start | bytes 1818632 | tf_op jit(solution)/shard_map/ppermute | solution.py:591
  64.7 40.3 %collective-permute-start.12 = (s16[592,512]{1,0:T(8,128)(2,1)}, s16[592,512]{1,0:T(8,128)(2,1)}, u32[]{:S(2)}, u32[]{:S(2)}) collective-permute-start(s16[592,512]{1,0:T(8,128)(2,1)} %get-tuple-element.54), channel_id=1, source_target_pairs={{0,4},{12,8},{1,5},{13,9},{2,6},{14,10},{3,7},{15,11},{16,20},{28,... | collective-permute-start | bytes 1818632 | tf_op jit(solution)/shard_map/ppermute | solution.py:591
  94.5 24.5 %copy-start.30 = (f32[8,576]{1,0:T(8,128)}, f32[8,576]{1,0:T(8,128)S(1)}, u32[]{:S(2)}) copy-start(f32[8,576]{1,0:T(8,128)S(1)} %bitcast_reduce_fusion) | copy-start | bytes 55300
  100.1 43.0 %collective-permute-start.15 = (s16[592,512]{1,0:T(8,128)(2,1)}, s16[592,512]{1,0:T(8,128)(2,1)S(1)}, u32[]{:S(2)}, u32[]{:S(2)}) collective-permute-start(s16[592,512]{1,0:T(8,128)(2,1)} %copy-done.26), channel_id=1, source_target_pairs={{0,4},{12,8},{1,5},{13,9},{2,6},{14,10},{3,7},{15,11},{16,20},{28,... | collective-permute-start | bytes 1818632 | tf_op jit(solution)/shard_map/ppermute | solution.py:591
  101.4 43.8 %collective-permute-start.7 = (s16[592,512]{1,0:T(8,128)(2,1)}, s16[592,512]{1,0:T(8,128)(2,1)}, u32[]{:S(2)}, u32[]{:S(2)}) collective-permute-start(s16[592,512]{1,0:T(8,128)(2,1)} %get-tuple-element.48), channel_id=1, source_target_pairs={{4,8},{8,4},{5,9},{9,5},{6,10},{10,6},{7,11},{11,7},{20,24},{24,20... | collective-permute-start | bytes 1818632 | tf_op jit(solution)/shard_map/ppermute | solution.py:602
  103.7 59.4 %collective-permute-start.4 = (s16[592,512]{1,0:T(8,128)(2,1)}, s16[592,512]{1,0:T(8,128)(2,1)}, u32[]{:S(2)}, u32[]{:S(2)}) collective-permute-start(s16[592,512]{1,0:T(8,128)(2,1)} %copy-done.29), channel_id=1, source_target_pairs={{4,8},{5,9},{6,10},{7,11},{20,24},{21,25},{22,26},{23,27}} | collective-permute-start | bytes 1818632 | tf_op jit(solution)/shard_map/ppermute | solution.py:605
  112.3 52.0 %collective-permute-start.21 = (s16[592,512]{1,0:T(8,128)(2,1)}, s16[592,512]{1,0:T(8,128)(2,1)S(1)}, u32[]{:S(2)}, u32[]{:S(2)}) collective-permute-start(s16[592,512]{1,0:T(8,128)(2,1)} %copy-done.25), channel_id=1, source_target_pairs={{0,4},{12,8},{1,5},{13,9},{2,6},{14,10},{3,7},{15,11},{16,20},{28,... | collective-permute-start | bytes 1818632 | tf_op jit(solution)/shard_map/ppermute | solution.py:591
  113.6 20.0 %copy-start.23 = (s16[592,512]{1,0:T(8,128)(2,1)}, s16[592,512]{1,0:T(8,128)(2,1)S(1)}, u32[]{:S(2)}) copy-start(s16[592,512]{1,0:T(8,128)(2,1)S(1)} %collective-permute-done.1.got_ref) | copy-start | bytes 1818628
  113.6 44.3 %collective-permute-start.13 = (s16[592,512]{1,0:T(8,128)(2,1)}, s16[592,512]{1,0:T(8,128)(2,1)}, u32[]{:S(2)}, u32[]{:S(2)}) collective-permute-start(s16[592,512]{1,0:T(8,128)(2,1)} %get-tuple-element.56), channel_id=1, source_target_pairs={{4,8},{8,4},{5,9},{9,5},{6,10},{10,6},{7,11},{11,7},{20,24},{24,20... | collective-permute-start | bytes 1818632 | tf_op jit(solution)/shard_map/ppermute | solution.py:602
  140.4 18.8 %slice-start = ((s8[4718592]{0:T(1024)(128)(4,1)}), s8[524288]{0:T(1024)(128)(4,1)S(1)}, s32[]{:S(2)}) async-start(s8[4718592]{0:T(1024)(128)(4,1)} %bitcast.32), calls=%async_computation.5 | async-start | bytes 1048576
  143.1 34.7 %collective-permute-start.2 = (s16[592,512]{1,0:T(8,128)(2,1)}, s16[592,512]{1,0:T(8,128)(2,1)}, u32[]{:S(2)}, u32[]{:S(2)}) collective-permute-start(s16[592,512]{1,0:T(8,128)(2,1)} %get-tuple-element.41), channel_id=1, source_target_pairs={{8,12},{4,0},{9,13},{5,1},{10,14},{6,2},{11,15},{7,3},{24,28},{20,... | collective-permute-start | bytes 1818632 | tf_op jit(solution)/shard_map/ppermute | solution.py:604
  145.2 33.9 %collective-permute-start.10 = (s16[592,512]{1,0:T(8,128)(2,1)}, s16[592,512]{1,0:T(8,128)(2,1)}, u32[]{:S(2)}, u32[]{:S(2)}) collective-permute-start(s16[592,512]{1,0:T(8,128)(2,1)} %copy-done.28), channel_id=1, source_target_pairs={{4,8},{5,9},{6,10},{7,11},{20,24},{21,25},{22,26},{23,27}} | collective-permute-start | bytes 1818632 | tf_op jit(solution)/shard_map/ppermute | solution.py:605
  157.9 32.8 %collective-permute-start.8 = (s16[592,512]{1,0:T(8,128)(2,1)S(1)}, s16[592,512]{1,0:T(8,128)(2,1)S(1)}, u32[]{:S(2)}, u32[]{:S(2)}) collective-permute-start(s16[592,512]{1,0:T(8,128)(2,1)S(1)} %get-tuple-element.49), channel_id=1, source_target_pairs={{8,12},{4,0},{9,13},{5,1},{10,14},{6,2},{11,15},{7,3},{24,28},{20,... | collective-permute-start | bytes 1818632 | tf_op jit(solution)/shard_map/ppermute | solution.py:604
  159.3 18.5 %copy-start.22 = (s16[592,512]{1,0:T(8,128)(2,1)S(1)}, s16[592,512]{1,0:T(8,128)(2,1)}, u32[]{:S(2)}) copy-start(s16[592,512]{1,0:T(8,128)(2,1)} %copy-done.21) | copy-start | bytes 1818628
  159.3 36.6 %slice-start.2 = ((s8[4718592]{0:T(1024)(128)(4,1)}), s8[4194304]{0:T(1024)(128)(4,1)S(1)}, s32[]{:S(2)}) async-start(s8[4718592]{0:T(1024)(128)(4,1)} %bitcast.34), calls=%async_computation.7 | async-start | bytes 8388608
  163.0 19.3 %copy-start.36 = (s32[16]{0:T(128)S(1)}, s32[16]{0:T(128)}, u32[]{:S(2)}) copy-start(s32[16]{0:T(128)} %param.24) | copy-start | bytes 196
  163.0 19.4 %copy-start.34 = (f32[512]{0:T(512)S(1)}, f32[512]{0:T(512)}, u32[]{:S(2)}) copy-start(f32[512]{0:T(512)} %param.18) | copy-start | bytes 6148
  163.1 36.7 %collective-permute-start.16 = (s16[592,512]{1,0:T(8,128)(2,1)S(1)}, s16[592,512]{1,0:T(8,128)(2,1)S(1)}, u32[]{:S(2)}, u32[]{:S(2)}) collective-permute-start(s16[592,512]{1,0:T(8,128)(2,1)S(1)} %get-tuple-element.60), channel_id=1, source_target_pairs={{4,8},{5,9},{6,10},{7,11},{20,24},{21,25},{22,26},{23,27}} | collective-permute-start | bytes 1818632 | tf_op jit(solution)/shard_map/ppermute | solution.py:605
  164.4 39.3 %collective-permute-start.14 = (s16[592,512]{1,0:T(8,128)(2,1)S(1)}, s16[592,512]{1,0:T(8,128)(2,1)S(1)}, u32[]{:S(2)}, u32[]{:S(2)}) collective-permute-start(s16[592,512]{1,0:T(8,128)(2,1)S(1)} %get-tuple-element.57), channel_id=1, source_target_pairs={{8,12},{4,0},{9,13},{5,1},{10,14},{6,2},{11,15},{7,3},{24,28},{20,... | collective-permute-start | bytes 1818632 | tf_op jit(solution)/shard_map/ppermute | solution.py:604
  169.1 26.8 %slice-start.3 = ((s8[4718592]{0:T(1024)(128)(4,1)}), s8[524288]{0:T(1024)(128)(4,1)S(1)}, s32[]{:S(2)}) async-start(s8[4718592]{0:T(1024)(128)(4,1)} %bitcast.34), calls=%async_computation.8 | async-start | bytes 1048576
  177.8 33.7 %collective-permute-start.23 = (s16[592,512]{1,0:T(8,128)(2,1)S(1)}, s16[592,512]{1,0:T(8,128)(2,1)S(1)}, u32[]{:S(2)}, u32[]{:S(2)}) collective-permute-start(s16[592,512]{1,0:T(8,128)(2,1)S(1)} %copy-done.22), channel_id=1, source_target_pairs={{0,4},{12,8},{1,5},{13,9},{2,6},{14,10},{3,7},{15,11},{16,20},{28,... | collective-permute-start | bytes 1818632 | tf_op jit(solution)/shard_map/ppermute | solution.py:591
  179.1 37.2 %collective-permute-start.22 = (s16[592,512]{1,0:T(8,128)(2,1)S(1)}, s16[592,512]{1,0:T(8,128)(2,1)S(1)}, u32[]{:S(2)}, u32[]{:S(2)}) collective-permute-start(s16[592,512]{1,0:T(8,128)(2,1)S(1)} %get-tuple-element.67), channel_id=1, source_target_pairs={{8,4},{9,5},{10,6},{11,7},{24,20},{25,21},{26,22},{27,23}} | collective-permute-start | bytes 1818632 | tf_op jit(solution)/shard_map/ppermute | solution.py:629
  190.7 35.7 %collective-permute-start.5 = (bf16[576,512]{1,0:T(8,128)(2,1)}, bf16[576,512]{1,0:T(8,128)(2,1)}, u32[]{:S(2)}, u32[]{:S(2)}) collective-permute-start(bf16[576,512]{1,0:T(8,128)(2,1)} %finish.3.refs_3_.keys_ref), channel_id=1, source_target_pairs={{8,12},{9,13},{10,14},{11,15},{24,28},{25,29},{26,30},{27,31}} | collective-permute-start | bytes 1769480 | tf_op jit(solution)/shard_map/ppermute | solution.py:608
  199.8 29.3 %collective-permute-start.11 = (bf16[576,512]{1,0:T(8,128)(2,1)}, bf16[576,512]{1,0:T(8,128)(2,1)}, u32[]{:S(2)}, u32[]{:S(2)}) collective-permute-start(bf16[576,512]{1,0:T(8,128)(2,1)} %finish.4.refs_4_.keys_ref), channel_id=1, source_target_pairs={{8,12},{9,13},{10,14},{11,15},{24,28},{25,29},{26,30},{27,31}} | collective-permute-start | bytes 1769480 | tf_op jit(solution)/shard_map/ppermute | solution.py:608
  203.7 14.1 %slice-start.4 = ((s8[4718592]{0:T(1024)(128)(4,1)}), s8[4194304]{0:T(1024)(128)(4,1)S(1)}, s32[]{:S(2)}) async-start(s8[4718592]{0:T(1024)(128)(4,1)} %bitcast.36), calls=%async_computation.9 | async-start | bytes 8388608
  203.7 14.1 %slice-start.5 = ((s8[4718592]{0:T(1024)(128)(4,1)}), s8[524288]{0:T(1024)(128)(4,1)S(1)}, s32[]{:S(2)}) async-start(s8[4718592]{0:T(1024)(128)(4,1)} %bitcast.36), calls=%async_computation.10 | async-start | bytes 1048576
  206.1 33.3 %collective-permute-start.17 = (bf16[576,512]{1,0:T(8,128)(2,1)}, bf16[576,512]{1,0:T(8,128)(2,1)}, u32[]{:S(2)}, u32[]{:S(2)}) collective-permute-start(bf16[576,512]{1,0:T(8,128)(2,1)} %finish.5.refs_5_.keys_ref), channel_id=1, source_target_pairs={{8,12},{9,13},{10,14},{11,15},{24,28},{25,29},{26,30},{27,31}} | collective-permute-start | bytes 1769480 | tf_op jit(solution)/shard_map/ppermute | solution.py:608
  214.2 34.4 %collective-permute-start.24 = (s16[592,512]{1,0:T(8,128)(2,1)}, s16[592,512]{1,0:T(8,128)(2,1)}, u32[]{:S(2)}, u32[]{:S(2)}) collective-permute-start(s16[592,512]{1,0:T(8,128)(2,1)} %get-tuple-element.69), channel_id=1, source_target_pairs={{8,4},{9,5},{10,6},{11,7},{24,20},{25,21},{26,22},{27,23}} | collective-permute-start | bytes 1818632 | tf_op jit(solution)/shard_map/ppermute | solution.py:629
  216.3 39.1 %collective-permute-start.25 = (s16[592,512]{1,0:T(8,128)(2,1)}, s16[592,512]{1,0:T(8,128)(2,1)S(1)}, u32[]{:S(2)}, u32[]{:S(2)}) collective-permute-start(s16[592,512]{1,0:T(8,128)(2,1)} %get-tuple-element.70), channel_id=1, source_target_pairs={{0,4},{12,8},{1,5},{13,9},{2,6},{14,10},{3,7},{15,11},{16,20},{28,... | collective-permute-start | bytes 1818632 | tf_op jit(solution)/shard_map/ppermute | solution.py:591
  222.1 26.6 %copy-start.18 = (s16[592,512]{1,0:T(8,128)(2,1)S(1)}, s16[592,512]{1,0:T(8,128)(2,1)}, u32[]{:S(2)}) copy-start(s16[592,512]{1,0:T(8,128)(2,1)} %copy-done.17) | copy-start | bytes 1818628
  222.1 53.1 %all-to-all-start.1 = ((bf16[4,128,576]{1,2,0:T(8,128)(2,1)}), bf16[4,128,576]{1,2,0:T(8,128)(2,1)}, u32[]{:S(2)}, u32[]{:S(2)}) async-start(bf16[4,128,576]{1,2,0:T(8,128)(2,1)} %copy.42), calls=%async_computation.1 | async-start | bytes 1179648 | tf_op jit(solution)/shard_map/all_to_all | solution.py:641
  244.5 16.3 %collective-permute-start.18 = (bf16[4,64,512]{2,1,0:T(8,128)(2,1)}, bf16[4,64,512]{2,1,0:T(8,128)(2,1)}, u32[]{:S(2)}, u32[]{:S(2)}) collective-permute-start(bf16[4,64,512]{2,1,0:T(8,128)(2,1)} %get-tuple-element.62), channel_id=1, source_target_pairs={{12,0},{13,1},{14,2},{15,3},{28,16},{29,17},{30,18},{31,19}} | collective-permute-start | bytes 786440 | tf_op jit(solution)/shard_map/ppermute | solution.py:611
  245.9 14.9 %collective-permute-start.19 = (bf16[4,64,512]{2,1,0:T(8,128)(2,1)S(1)}, bf16[4,64,512]{2,1,0:T(8,128)(2,1)}, u32[]{:S(2)}, u32[]{:S(2)}) collective-permute-start(bf16[4,64,512]{2,1,0:T(8,128)(2,1)S(1)} %get-tuple-element.63), channel_id=1, source_target_pairs={{12,4},{13,5},{14,6},{15,7},{28,20},{29,21},{30,22},{31,23}} | collective-permute-start | bytes 786440 | tf_op jit(solution)/shard_map/ppermute | solution.py:611
  247.3 19.5 %collective-permute-start.20 = (bf16[4,64,512]{2,1,0:T(8,128)(2,1)S(1)}, bf16[4,64,512]{2,1,0:T(8,128)(2,1)}, u32[]{:S(2)}, u32[]{:S(2)}) collective-permute-start(bf16[4,64,512]{2,1,0:T(8,128)(2,1)S(1)} %get-tuple-element.64), channel_id=1, source_target_pairs={{12,8},{13,9},{14,10},{15,11},{28,24},{29,25},{30,26},{31,27}} | collective-permute-start | bytes 786440 | tf_op jit(solution)/shard_map/ppermute | solution.py:611
  259.4 32.8 %collective-permute-start.26 = (s16[592,512]{1,0:T(8,128)(2,1)S(1)}, s16[592,512]{1,0:T(8,128)(2,1)S(1)}, u32[]{:S(2)}, u32[]{:S(2)}) collective-permute-start(s16[592,512]{1,0:T(8,128)(2,1)S(1)} %get-tuple-element.71), channel_id=1, source_target_pairs={{8,4},{9,5},{10,6},{11,7},{24,20},{25,21},{26,22},{27,23}} | collective-permute-start | bytes 1818632 | tf_op jit(solution)/shard_map/ppermute | solution.py:629
  275.2 13.8 %all-to-all-start.2 = ((bf16[4,128,576]{1,2,0:T(8,128)(2,1)}), bf16[4,128,576]{1,2,0:T(8,128)(2,1)}, u32[]{:S(2)}, u32[]{:S(2)}) async-start(bf16[4,128,576]{1,2,0:T(8,128)(2,1)} %copy.43), calls=%async_computation.2 | async-start | bytes 1179648 | tf_op jit(solution)/shard_map/all_to_all | solution.py:641
  289.0 10.0 %all-to-all-start = ((bf16[4,2,4096]{2,1,0:T(2,128)(2,1)}), bf16[4,2,4096]{2,1,0:T(2,128)(2,1)S(1)}, u32[]{:S(2)}, u32[]{:S(2)}) async-start(bf16[4,2,4096]{2,1,0:T(2,128)(2,1)} %select_convert_fusion), calls=%async_computation | async-start | bytes 131072 | tf_op jit(solution)/shard_map/all_to_all | solution.py:625
  294.6 20.0 %copy-start.1 = (bf16[16,2,1536]{2,1,0:T(2,128)(2,1)S(1)}, bf16[16,2,1536]{2,1,0:T(2,128)(2,1)}, u32[]{:S(2)}) copy-start(bf16[16,2,1536]{2,1,0:T(2,128)(2,1)} %param.19) | copy-start | bytes 294916
  298.9 13.0 %all-to-all-start.3 = ((bf16[4,128,576]{1,2,0:T(8,128)(2,1)}), bf16[4,128,576]{1,2,0:T(8,128)(2,1)S(1)}, u32[]{:S(2)}, u32[]{:S(2)}) async-start(bf16[4,128,576]{1,2,0:T(8,128)(2,1)} %copy.44), calls=%async_computation.3 | async-start | bytes 1179648 | tf_op jit(solution)/shard_map/all_to_all | solution.py:641
  (31 other events, 155.6 us)
Sparse Core Ops, SparseCore 0:
  134.7 39.6 all-gather.2
